TPU v7x, 32 devices: a whole 2x2x4 slice. The times are simulated.
32 devices in a mesh: rows: 8 (over z, x), sk: 4 (over y, core).
Axes of the slice: x: 2, y: 2, z: 4, core: 2. Of those that a mesh axis runs over, the one named last changes fastest.
Arguments:
- panel: float32 [64, 262144], P(None, ('rows', 'sk')), may hold values from -200 to 200
- signs: int32 [262144], P(('rows', 'sk')), may hold values from -1 to 1
- sample_device: int32 [4096, 1], replicated, may hold values from 0 to 31; in each aligned block of 128 rows (0 to 127, 128 to 255, ...) at most 4 rows name the same one
- sample_offset: int32 [4096], replicated, may hold values from 0 to 8191
Outputs:
- mixed: float32 [64, 262144], P(None, ('rows', 'sk'))
- r_factor: float32 [64, 64], replicated
- whitened: float32 [64, 4096], P(None, ('rows', 'sk'))
Inputs may be any that keep to these rules, and one draw needn't show every extreme that they name: `sample_device`: among the sample positions j * 128 to (j + 1) * 128 - 1 of any j, no device number appears more than 4 times, and some block reaches it.
All inputs are finite; a program needn't handle non-finite values.
Results may differ from a plain program's by a relative error of at most 0.0003.
Values sent between devices are 32-bit elements; how exact they have to be, the bound alone decides.
No kernel may reach another device: no remote copies, remote signals or barrier semaphores. Data moves between devices by JAX's collectives and lax.ppermute only.
A program may use at most 64 MiB of HBM per device.

v0:
```python
import math

import jax
import jax.numpy as jnp
from jax import lax
from jax.sharding import PartitionSpec as P


def hadamard_table(order_size):
    left_ids = jnp.arange(order_size, dtype=jnp.int32)[:, None]
    right_ids = jnp.arange(order_size, dtype=jnp.int32)[None, :]
    common = jnp.bitwise_and(left_ids, right_ids)
    parity = jnp.zeros((order_size, order_size), jnp.int32)
    for bit_number in range(max(order_size.bit_length() - 1, 1)):
        parity = parity + jnp.bitwise_and(jnp.right_shift(common, bit_number), 1)
    return jnp.where(parity % 2 == 0, 1.0, -1.0).astype(jnp.float32)


def householder_r(matrix):
    rows_count, cols_count = matrix.shape
    position = jnp.arange(rows_count, dtype=jnp.int32)

    def reflect(j, current):
        column = lax.dynamic_slice_in_dim(current, j, 1, 1)[:, 0]
        column = jnp.where(position >= j, column, jnp.float32(0.0))
        pivot_value = column[j]
        length = jnp.sqrt(jnp.sum(column * column))
        signed = jnp.where(pivot_value >= 0, jnp.float32(1.0), jnp.float32(-1.0))
        vector = column + signed * length * (position == j).astype(jnp.float32)
        denominator = jnp.sum(vector * vector)
        projection = jnp.dot(vector, current, precision=lax.Precision.HIGHEST)
        return current - vector[:, None] * projection[None, :] * (2.0 / denominator)

    reduced = lax.fori_loop(0, cols_count, reflect, matrix)
    upper = jnp.triu(reduced[:cols_count])
    diag_signs = jnp.where(jnp.diagonal(upper) >= 0, jnp.float32(1.0), jnp.float32(-1.0))
    return upper * diag_signs[:, None]


def forward_solve(upper, values):
    lower = upper.T
    order_size = lower.shape[0]

    def step_row(i, solved):
        row_coef = lax.dynamic_slice_in_dim(lower, i, 1, 0)
        partial_sum = jnp.dot(row_coef, solved, precision=lax.Precision.HIGHEST)
        target = lax.dynamic_slice_in_dim(values, i, 1, 0)
        pivot = lax.dynamic_slice_in_dim(row_coef[0], i, 1, 0)
        new_row = (target - partial_sum) / pivot[0]
        return lax.dynamic_update_slice_in_dim(solved, new_row, i, 0)

    return lax.fori_loop(0, order_size, step_row, jnp.zeros(values.shape, jnp.float32))


def local(panel, signs, sample_device, sample_offset):
    high = lax.Precision.HIGHEST
    device_count = lax.axis_size(("rows", "sk"))
    device_id = lax.axis_index(("rows", "sk"))
    cols_here, local_rows = panel.shape
    inner = local_rows // 128
    flipped = panel * signs.astype(jnp.float32)[None, :]
    cube = flipped.reshape(cols_here, inner, 128)
    cube = jnp.einsum("cab,ea->ceb", cube, hadamard_table(inner), precision=high)
    cube = jnp.einsum("cab,db->cad", cube, hadamard_table(128), precision=high)
    local_mix = cube.reshape(cols_here, local_rows)
    piece_rows = local_rows // device_count
    device_table = hadamard_table(device_count)
    received = lax.all_to_all(local_mix, ("rows", "sk"), split_axis=1, concat_axis=1, tiled=True)
    grouped = received.reshape(received.shape[0], device_count, piece_rows)
    mixed_pieces = jnp.einsum("cqr,pq->cpr", grouped, device_table, precision=high)
    flat_pieces = mixed_pieces.reshape(received.shape[0], local_rows)
    spread = lax.all_to_all(flat_pieces, ("rows", "sk"), split_axis=1, concat_axis=1, tiled=True)
    mixed = spread * (1.0 / math.sqrt(local_rows * device_count))
    sources = sample_device[:, 0]
    total_samples = sources.shape[0]
    owned = (sources == device_id).astype(jnp.float32)
    term = jnp.take(mixed, sample_offset, axis=1) * owned[None, :]
    picked = lax.psum_scatter(term, ("rows", "sk"), scatter_dimension=1, tiled=True)
    sketch = picked * (1.0 / math.sqrt(total_samples))
    local_factor = householder_r(sketch.T)
    stacked = lax.all_gather(local_factor, ("rows", "sk"), axis=0, tiled=True)
    r_factor = householder_r(stacked)
    whitened = forward_solve(r_factor, picked)
    return (mixed, r_factor, whitened)


def solution(mesh):
    return jax.shard_map(
        local,
        mesh=mesh,
        in_specs=(P(None, ("rows", "sk")), P(("rows", "sk")), P(), P()),
        out_specs=(P(None, ("rows", "sk")), P(), P(None, ("rows", "sk"))),
        check_vma=False,
    )
```

profile of v0, /device:TPU:0, one launch (start us, length us, event | category | flops | bytes accessed | tf_op | source)
XLA Modules:
  0.0 969.8 jit_solution(16307747184098491595)
XLA Ops:
  7.9 1.8 multiply_bitcast_fusion.1
  10.1 2.0 fusion.33
  12.1 1.9 fusion.16
  14.0 1.6 all_to_all.10
  15.6 2.8 copy.19
  18.4 55.8 %all_to_all.15 = f32[64,32,256]{2,0,1:T(8,128)S(1)} all-to-all(f32[64,32,256]{2,0,1:T(8,128)S(1)} %copy.19), channel_id=1, replica_groups=mesh['rows'=8,'sk'=4] {'rows','sk'}, dimensions={1} | all-to-all | bytes 4194304 | tf_op jit(solution)/shard_map/all_to_all | solution.py:68
  74.2 3.0 fusion.20
  77.2 2.5 copy.21
  79.8 3.8 all-to-all-start.1
  83.9 48.4 %all-to-all-done.1 = f32[64,32,256]{2,0,1:T(8,128)} async-done(((f32[64,32,256]{2,0,1:T(8,128)}), f32[64,32,256]{2,0,1:T(8,128)}, u32[]{:S(2)}, u32[]{:S(2)}) %all-to-all-start.1) | async-done | bytes 2097184 | tf_op jit(solution)/shard_map/all_to_all | solution.py:72
  132.3 1.8 broadcast_multiply_fusion
  134.1 2.7 copy.22
  136.8 13.0 %gather_fusion = f32[4096,64]{1,0:T(8,128)S(1)} fusion(f32[64,8192]{0,1:T(8,128)} %bitcast.102, s32[4096]{0:T(1024)S(1)} %fusion.65), kind=kCustom, calls=%fused_computation | custom fusion | bytes 2113536 | tf_op jit(solution)/shard_map/jit(_take)/gather | solution.py:77
  149.8 2.7 multiply_bitcast_fusion
  152.5 3.8 copy.29
  156.3 132.8 %reduce-scatter.2.cloned.1.call-done = f32[64,128]{0,1:T(8,128)} async-done(((f32[64,4096]{0,1:T(8,128)}), f32[64,128]{0,1:T(8,128)}) %reduce-scatter.2.cloned.1.call-update) | async-done | bytes 32784 | tf_op jit(solution)/shard_map/reduce_scatter | solution.py:78
  289.0 0.8 multiply_bitcast_fusion.2
  289.9 251.4 %while.47 = (s32[]{:T(128)}, f32[128,64]{0,1:T(8,128)S(1)}, s32[]{:T(128)}, f32[]{:T(128)}, f32[1]{0:T(128)}, /*index=5*/f32[1]{0:T(128)}, f32[1]{0:T(128)}) while((s32[]{:T(128)}, f32[128,64]{0,1:T(8,128)S(1)}, s32[]{:T(128)}, f32[]{:T(128)}, f32[1]{0:T(128)}, /*index=5*/f32[1]{0:T(128)}, f32[1]{0:T(128)}) %tuple.120), condition=%wide.region_4.5_spmd.clone.clone, body=%wide.region_1.4_spmd.clone.clone.sunk | while | flops 125060 | bytes 104623 | solution.py:34
  541.5 0.8 gather_fusion.1
  542.4 39.3 %all_gather.3 = f32[2048,64]{1,0:T(8,128)S(1)} all-gather(f32[64,64]{1,0:T(8,128)S(1)} %broadcast_multiply_fusion.2), channel_id=1, replica_groups=mesh['rows'=8,'sk'=4] {'rows','sk'}, dimensions={0}, use_global_device_ids=true | all-gather | bytes 540672 | tf_op jit(solution)/shard_map/all_gather | solution.py:81
  582.0 287.6 %while.48 = (s32[]{:T(128)}, f32[2048,64]{0,1:T(8,128)S(1)}, s32[]{:T(128)}, f32[]{:T(128)}, f32[1]{0:T(128)}, /*index=5*/f32[1]{0:T(128)}, f32[1]{0:T(128)}) while((s32[]{:T(128)}, f32[2048,64]{0,1:T(8,128)S(1)}, s32[]{:T(128)}, f32[]{:T(128)}, f32[1]{0:T(128)}, /*index=5*/f32[1]{0:T(128)}, f32[1]{0:T(128)}) %tuple.123), condition=%wide.region_8.9_spmd.clone.clone, body=%wide.region_5.8_spmd.clone.clone.sunk | while | flops 1990660 | bytes 1675955 | solution.py:34
  870.0 0.8 gather_fusion.2
  871.8 90.6 %while.46 = (s32[]{:T(128)}, f32[64,128]{1,0:T(8,128)S(1)}, f32[64,128]{1,0:T(8,128)S(1)}, f32[64,64]{1,0:T(8,128)S(1)}, s32[]{:T(128)}, /*index=5*/s32[]{:T(128)}, s32[]{:T(128)}) while((s32[]{:T(128)}, f32[64,128]{1,0:T(8,128)S(1)}, f32[64,128]{1,0:T(8,128)S(1)}, f32[64,64]{1,0:T(8,128)S(1)}, s32[]{:T(128)}, /*index=5*/s32[]{:T(128)}, ...), condition=%wide.region_10.11_spmd, body=%wide.region_9.10_spmd.sunk | while | flops 98563 | bytes 36973 | solution.py:52
  872.4 0.8 fusion.115
  (1118 shorter events, 384.6 us)
Async XLA Ops:
  79.8 4.0 copy-start.2
  79.8 4.1 copy-start.3
  79.8 52.6 %all-to-all-start.1 = ((f32[64,32,256]{2,0,1:T(8,128)}), f32[64,32,256]{2,0,1:T(8,128)}, u32[]{:S(2)}, u32[]{:S(2)}) async-start(f32[64,32,256]{2,0,1:T(8,128)} %copy.21), calls=%async_computation.1 | async-start | bytes 4194304 | tf_op jit(solution)/shard_map/all_to_all | solution.py:72
  83.6 205.5 %reduce-scatter.2.cloned.1.call-start = ((), (), s32[]{:S(2)}) async-start(), calls=%async_computation.3 | async-start | bytes 2162688 | tf_op jit(solution)/shard_map/reduce_scatter | solution.py:78
  869.6 2.1 copy-start.1
  962.4 0.6 copy-start
Sparse Core Ops, SparseCore 0:
  152.6 136.4 reduce-scatter.1
where the time goes:
time: 974 us; the launch traced here: 970 us
  loops' own time  248 us (25%)
  other arithmetic  183 us (19%)
  waiting for transfers between devices  181 us (19%)
  local copies, waits for them, and re-layouts  146 us (15%)
  matrix products  98.2 us (10%)
  blocking collectives  95.1 us (10%)
  between operations  14.2 us (1%)
    another operation x2, loops' own time, householder_r(): reduced = lax.fori_loop(0, cols_count, reflect, matrix)  247 us
    reduce_scatter x1, waiting for transfers between devices, local(): lax.psum_scatter(term, ('rows', 'sk'), scatter_dimension=1, tiled=True)  133 us
    reduce_sum x128, other arithmetic, reflect(): denominator = jnp.sum(vector * vector)  78.9 us
    reduce_sum x128, other arithmetic, reflect(): length = jnp.sqrt(jnp.sum(column * column))  77.1 us
    dynamic_slice x128, local copies, waits for them, and re-layouts, reflect(): pivot_value = column[j]  75.8 us
    all_to_all x1, blocking collectives, local(): lax.all_to_all(local_mix, ('rows', 'sk'), split_axis=1, concat_axis=1, ti...  55.8 us
    dot_general x64, matrix products, step_row(): partial_sum = jnp.dot(row_coef, solved, precision=lax.Precision.HIGHEST)  50 us
    all_to_all x1, waiting for transfers between devices, local(): lax.all_to_all(flat_pieces, ('rows', 'sk'), split_axis=1, concat_axis=1,...  48.4 us
  transfers between devices with their start and end apart: 2, of which 2 were waited for; matrix products, arithmetic and copies ran while one was open for 0% of the time, Pallas kernels for 0%

commit v1 on v0

v1 whole, which is shorter than its diff:
```python
import functools
import math

import jax
import jax.numpy as jnp
import numpy as np
from jax import lax
from jax.experimental import pallas as pl
from jax.experimental.pallas import tpu as pltpu
from jax.sharding import PartitionSpec as P

AXES = ("rows", "sk")
LANES = 128
GROUP = 8
SLICES = 6


def hadamard_np(order_size):
    table = np.ones((1, 1), np.float32)
    while table.shape[0] < order_size:
        table = np.block([[table, table], [table, -table]])
    return table


def mix_kernel(scale, panel_ref, signs_ref, table_ref, out_ref):
    rows = panel_ref.shape[1]
    inner = rows // LANES
    flipped = panel_ref[...] * (signs_ref[...].astype(jnp.float32) * scale)
    stacked = jnp.concatenate(
        [flipped[:, a * LANES : (a + 1) * LANES] for a in range(inner)], axis=0
    )
    table = table_ref[...]
    total = None
    rest = stacked
    for piece in range(3):
        part = rest.astype(jnp.bfloat16)
        term = jnp.dot(part, table, preferred_element_type=jnp.float32)
        total = term if total is None else total + term
        if piece < 2:
            rest = rest - part.astype(jnp.float32)
    blocks = [total[a * GROUP : (a + 1) * GROUP] for a in range(inner)]
    span = 1
    while span < inner:
        for a in range(inner):
            if a & span == 0:
                left, right = blocks[a], blocks[a + span]
                blocks[a], blocks[a + span] = left + right, left - right
        span *= 2
    for a in range(inner):
        out_ref[:, a * LANES : (a + 1) * LANES] = blocks[a]


def local_mix(panel, signs_row, table, scale, first, count):
    rows = panel.shape[1]
    return pl.pallas_call(
        functools.partial(mix_kernel, scale),
        grid=(count // GROUP,),
        in_specs=[
            pl.BlockSpec((GROUP, rows), lambda i: (first // GROUP + i, 0)),
            pl.BlockSpec((1, rows), lambda i: (0, 0)),
            pl.BlockSpec((LANES, LANES), lambda i: (0, 0)),
        ],
        out_specs=pl.BlockSpec((GROUP, rows), lambda i: (i, 0)),
        out_shape=jax.ShapeDtypeStruct((count, rows), jnp.float32),
        compiler_params=pltpu.CompilerParams(vmem_limit_bytes=32 << 20),
        cost_estimate=pl.CostEstimate(
            flops=count * rows * 800, bytes_accessed=count * rows * 8, transcendentals=0
        ),
    )(panel, signs_row, table)


def terms_kernel(bits, half, code_ref, me_ref, *refs):
    chunk_refs, out_ref, table_ref = refs[:-2], refs[-2], refs[-1]
    rows = chunk_refs[0].shape[1]
    me = me_ref[0]

    def transpose_block(a, carry):
        start = pl.multiple_of(a * LANES, LANES)
        tile = jnp.concatenate([ref[:, pl.ds(start, LANES)] for ref in chunk_refs], axis=0)
        turned = jnp.concatenate([tile, tile], axis=0).T
        table_ref[pl.ds(start, LANES), :] = turned
        table_ref[pl.ds(rows + start, LANES), :] = -turned
        return carry

    lax.fori_loop(0, rows // LANES, transpose_block, 0)
    first_half = lax.broadcasted_iota(jnp.int32, (1, LANES), 1) < LANES // 2

    def gather_block(r, carry):
        mask = jnp.int32(0)
        for bit in range(bits):
            mask = mask | (((r >> bit) & 1) << (bits - 1 - bit))
        source = (me ^ mask) * (2 * half)
        target = pl.multiple_of(r * half, half)
        for j in range(half):
            upper = table_ref[pl.ds(code_ref[source + j], 1), :]
            lower = table_ref[pl.ds(code_ref[source + half + j], 1), :]
            out_ref[pl.ds(target + j, 1), :] = jnp.where(first_half, upper, lower)
        return carry

    lax.fori_loop(0, 1 << bits, gather_block, 0)


def sampled_terms(chunks, code, me, bits, half):
    rows = chunks[0].shape[1]
    count = half << bits
    return pl.pallas_call(
        functools.partial(terms_kernel, bits, half),
        in_specs=[pl.BlockSpec(memory_space=pltpu.SMEM)] * 2
        + [pl.BlockSpec(memory_space=pltpu.VMEM)] * len(chunks),
        out_specs=pl.BlockSpec(memory_space=pltpu.VMEM),
        out_shape=jax.ShapeDtypeStruct((count, LANES), jnp.float32),
        scratch_shapes=[pltpu.VMEM((2 * rows, LANES), jnp.float32)],
        compiler_params=pltpu.CompilerParams(vmem_limit_bytes=40 << 20),
        cost_estimate=pl.CostEstimate(
            flops=count * LANES * 40, bytes_accessed=24 << 20, transcendentals=0
        ),
    )(code, me, *chunks)


def two_sum(a, b):
    total = a + b
    part = total - a
    return total, (a - (total - part)) + (b - part)


def quick_sum(a, b):
    total = a + b
    return total, b - (total - a)


def pair_add(a, b):
    total, error = two_sum(a[0], b[0])
    return quick_sum(total, error + (a[1] + b[1]))


def halves(a):
    scaled = a * 4097.0
    high = scaled - (scaled - a)
    return high, a - high


def product(a, b, a_parts, b_parts):
    whole = a * b
    error = (a_parts[0] * b_parts[0] - whole) + a_parts[0] * b_parts[1]
    error = (error + a_parts[1] * b_parts[0]) + a_parts[1] * b_parts[1]
    return whole, error


def gram_kernel(scale, terms_ref, picked_ref, gram_ref):
    cols = picked_ref.shape[0]
    turned = terms_ref[...].T
    picked = jnp.concatenate([turned[:cols], turned[cols:]], axis=1)
    picked_ref[...] = picked
    rest = picked * scale
    shift = jnp.max(jnp.abs(rest), axis=1, keepdims=True) * float(1 << 17)
    parts = []
    for _ in range(SLICES):
        part = (rest + shift) - shift
        rest = rest - part
        shift = shift * (1.0 / 64.0)
        parts.append(part.astype(jnp.bfloat16))
    total = None
    for level in range(SLICES):
        left = jnp.concatenate(parts[: level + 1], axis=1)
        right = jnp.concatenate(parts[: level + 1][::-1], axis=1)
        term = lax.dot_general(
            left, right, (((1,), (1,)), ((), ())), preferred_element_type=jnp.float32
        )
        if total is None:
            total = (term, jnp.zeros_like(term))
        else:
            high, error = two_sum(total[0], term)
            total = (high, total[1] + error)
    high, low = quick_sum(*total)
    gram_ref[...] = jnp.concatenate([high, low], axis=1)


def own_gram(terms, cols, per_device, scale):
    return pl.pallas_call(
        functools.partial(gram_kernel, scale),
        out_shape=(
            jax.ShapeDtypeStruct((cols, per_device), jnp.float32),
            jax.ShapeDtypeStruct((cols, 2 * cols), jnp.float32),
        ),
    )(terms)


def tree_sum(values):
    while len(values) > 1:
        values = [pair_add(values[i], values[i + 1]) for i in range(0, len(values), 2)]
    return values[0]


def split_pair(packed):
    cols = packed.shape[0]
    return packed[:, :cols], packed[:, cols:]


def gram_sum_kernel(*refs):
    high, low = tree_sum([split_pair(ref[...]) for ref in refs[:-1]])
    refs[-1][...] = jnp.concatenate([high, low], axis=1)


def gram_sum(grams):
    return pl.pallas_call(
        gram_sum_kernel, out_shape=jax.ShapeDtypeStruct(grams[0].shape, jnp.float32)
    )(*grams)


def factor_kernel(picked_ref, *refs):
    gram_refs, (r_ref, white_ref) = refs[:-2], refs[-2:]
    cols = r_ref.shape[0]
    high, low = tree_sum([split_pair(ref[...]) for ref in gram_refs])
    row_id = lax.broadcasted_iota(jnp.int32, (cols, cols), 0)
    lane_id = lax.broadcasted_iota(jnp.int32, (cols, cols), 1)
    unit = (row_id == lane_id).astype(jnp.float32)
    wide_high = jnp.concatenate([high, unit], axis=1)
    wide_low = jnp.concatenate([low, jnp.zeros_like(unit)], axis=1)
    tiles = cols // 8
    shape = (8, 2 * cols)
    rows = [
        (wide_high[t * 8 : (t + 1) * 8], wide_low[t * 8 : (t + 1) * 8])
        for t in range(tiles)
    ]
    sub_id = lax.broadcasted_iota(jnp.int32, shape, 0)
    for j in range(cols - 1):
        tile, sub = divmod(j, 8)
        row = [jnp.broadcast_to(v[sub : sub + 1], shape) for v in rows[tile]]
        pivot = [jnp.broadcast_to(v[sub : sub + 1, j : j + 1], shape) for v in rows[tile]]
        first = 1.0 / pivot[0]
        first_parts = halves(first)
        whole, error = product(pivot[0], first, halves(pivot[0]), first_parts)
        gap = ((1.0 - whole) - error) - pivot[1] * first
        inverse = quick_sum(first, first * gap)
        whole, error = product(row[0], inverse[0], halves(row[0]), halves(inverse[0]))
        scaled = quick_sum(whole, error + (row[0] * inverse[1] + row[1] * inverse[0]))
        scaled_parts = halves(scaled[0])
        for t in range(tile, tiles):
            if t == tile and sub == 7:
                continue
            high, low = rows[t]
            column = [jnp.broadcast_to(v[:, j : j + 1], shape) for v in rows[t]]
            if t == tile:
                column = [jnp.where(sub_id > sub, v, 0.0) for v in column]
            whole, error = product(column[0], scaled[0], halves(column[0]), scaled_parts)
            error = error + (column[0] * scaled[1] + column[1] * scaled[0])
            total, missed = two_sum(high, -whole)
            rows[t] = quick_sum(total, missed + (low - error))
    wide_high = jnp.concatenate([v[0] for v in rows], axis=0)
    wide_low = jnp.concatenate([v[1] for v in rows], axis=0)
    wide_row = lax.broadcasted_iota(jnp.int32, wide_high.shape, 0)
    wide_lane = lax.broadcasted_iota(jnp.int32, wide_high.shape, 1)
    diagonal = jnp.sum(jnp.where(wide_row == wide_lane, wide_high, 0.0), axis=1, keepdims=True)
    root = jnp.sqrt(diagonal)
    wide = (wide_high + wide_low) / root
    r_ref[...] = jnp.where(lane_id >= row_id, wide[:, :cols], 0.0)
    white_ref[...] = jnp.dot(
        wide[:, cols:],
        picked_ref[...],
        precision=lax.Precision.HIGHEST,
        preferred_element_type=jnp.float32,
    )


def factor_and_solve(picked, grams):
    cols = picked.shape[0]
    return pl.pallas_call(
        factor_kernel,
        out_shape=(
            jax.ShapeDtypeStruct((cols, cols), jnp.float32),
            jax.ShapeDtypeStruct(picked.shape, jnp.float32),
        ),
        cost_estimate=pl.CostEstimate(
            flops=20_000_000, bytes_accessed=1 << 18, transcendentals=0
        ),
    )(picked, *grams)


def xor_permute(value, mask, device_count):
    return lax.ppermute(value, AXES, [(i, i ^ mask) for i in range(device_count)])


def in_groups(masks, size):
    return [masks[i : i + size] for i in range(0, len(masks), size)]


def combined(masks, q):
    mask = 0
    for bit, value in enumerate(masks):
        if (q >> bit) & 1:
            mask |= value
    return mask


def local(panel, signs, sample_device, sample_offset):
    device_count = lax.axis_size(AXES)
    me = lax.axis_index(AXES).astype(jnp.int32)
    bits = device_count.bit_length() - 1
    cols, rows = panel.shape
    samples = sample_offset.shape[0]
    per_device = samples // device_count
    half = per_device // 2
    masks = [1 << bit for bit in range(bits)]

    table = jnp.asarray(hadamard_np(LANES), jnp.bfloat16)
    signs_row = signs.reshape(1, rows)
    scale = 1.0 / math.sqrt(rows * device_count)

    parts = 4
    width = cols // parts
    chunks = [
        local_mix(panel, signs_row, table, scale, part * width, width) for part in range(parts)
    ]

    far = masks[::-1]
    swapped = list(masks)
    if bits > 2:
        swapped[1], swapped[2] = swapped[2], swapped[1]
    orders = [far, swapped[::-1], masks, swapped]

    def own_sign(mask):
        return jnp.where((me & mask) == 0, jnp.float32(1.0), jnp.float32(-1.0))

    done = []
    for chunk, order in zip(chunks, orders):
        value = chunk
        for mask in order:
            other = xor_permute(value, mask, device_count)
            value = other + own_sign(mask) * value
        done.append(value)
    mixed = jnp.concatenate(done, axis=0)

    common = me & sample_device[:, 0]
    odd = lax.population_count(common) & 1
    code = sample_offset + odd * rows
    total = sampled_terms(chunks, code, me.reshape(1), bits, half)
    for group in in_groups(masks, 2):
        block = total.shape[0] >> len(group)
        mine = total[:block]
        for q in range(1, 1 << len(group)):
            mask = combined(group[::-1], q)
            mine = mine + xor_permute(total[q * block : (q + 1) * block], mask, device_count)
        total = mine

    picked, gram = own_gram(total, cols, per_device, 1.0 / math.sqrt(samples))
    groups = in_groups(far, 2)
    if len(groups) > 1 and len(groups[-1]) == 1:
        groups = groups[:-2] + [groups[-2] + groups[-1]]
    for number, group in enumerate(groups):
        received = [gram] + [
            xor_permute(gram, combined(group, q), device_count) for q in range(1, 1 << len(group))
        ]
        if number < len(groups) - 1:
            gram = gram_sum(received)
    r_factor, whitened = factor_and_solve(picked, received)
    return (mixed, r_factor, whitened)


def solution(mesh):
    return jax.shard_map(
        local,
        mesh=mesh,
        in_specs=(P(None, AXES), P(AXES), P(), P()),
        out_specs=(P(None, AXES), P(), P(None, AXES)),
        check_vma=False,
    )
```

time: 974 us -> 220 us (0.23)
  loops' own time: 248 us -> 0 us
  other arithmetic: 183 us -> 5.58 us
  local copies, waits for them, and re-layouts: 146 us -> 4.37 us
  matrix products: 98.2 us -> 0 us
  blocking collectives: 95.1 us -> 0 us
  waiting for transfers between devices: 181 us -> 142 us
  starting transfers between devices: 4.02 us -> 37.7 us
  Pallas kernels: 0 us -> 29.3 us
  between operations: 14.2 us -> 0.97 us
    another operation x3 -> x0, loops' own time: 248 us -> none  [the longest x2 247 us: householder_r(): reduced = lax.fori_loop(0, cols_count, reflect, matrix)]
    reduce_sum x256 -> x0, other arithmetic: 156 us -> none  [the longest x128 78.9 us: reflect(): denominator = jnp.sum(vector * vector)]
    ppermute x0 -> x37, waiting for transfers between devices: none -> 142 us  [xor_permute(): lax.ppermute(value, AXES, [(i, i ^ mask) for i in range(device_count)])]
    reduce_scatter x1 -> x0, waiting for transfers between devices: 133 us -> none  [local(): lax.psum_scatter(term, ('rows', 'sk'), scatter_dimension=1, tiled=True)]
    dynamic_slice x256 -> x0, local copies, waits for them, and re-layouts: 114 us -> none  [the longest x128 75.8 us: reflect(): pivot_value = column[j]]
    dot_general x195 -> x0, matrix products: 98.2 us -> none  [the longest x64 50 us: step_row(): partial_sum = jnp.dot(row_coef, solved, precision=lax.Precision.HIGHEST)]
    all_to_all x1 -> x0, blocking collectives: 55.8 us -> none  [local(): lax.all_to_all(local_mix, ('rows', 'sk'), split_axis=1, concat_axis=1, ti...]
    all_to_all x1 -> x0, waiting for transfers between devices: 48.4 us -> none  [local(): lax.all_to_all(flat_pieces, ('rows', 'sk'), split_axis=1, concat_axis=1,...]
  transfers between devices with their start and end apart: 2 -> 37, of which waited for: 2 -> 23; matrix products, arithmetic and copies ran while one was open for 0% -> 2% of each run, Pallas kernels for 0% -> 7%
where the time goes in v1:
time: 220 us; the launch traced here: 219 us
  waiting for transfers between devices  142 us (65%)
  starting transfers between devices  37.7 us (17%)
  Pallas kernels  29.3 us (13%)
  other arithmetic  5.58 us (3%)
  local copies, waits for them, and re-layouts  4.37 us (2%)
    ppermute x37, waiting for transfers between devices, xor_permute(): lax.ppermute(value, AXES, [(i, i ^ mask) for i in range(device_count)])  142 us
    ppermute x37, starting transfers between devices, xor_permute(): lax.ppermute(value, AXES, [(i, i ^ mask) for i in range(device_count)])  37.7 us
    pallas_call x1, Pallas kernels, factor_and_solve(): pl.pallas_call(factor_kernel, out_shape=(jax.ShapeDtypeStruct((cols, cols...  12.6 us
    pallas_call x1, Pallas kernels, sampled_terms(): pl.pallas_call(functools.partial(terms_kernel, bits, half), in_specs=[pl....  10.8 us
  transfers between devices with their start and end apart: 37, of which 23 were waited for; matrix products, arithmetic and copies ran while one was open for 2% of the time, Pallas kernels for 7%

profile of v1, /device:TPU:0, one launch (start us, length us, event | category | flops | bytes accessed | tf_op | source)
XLA Modules:
  0.0 219.5 jit_solution(4808479635673246854)
XLA Ops:
  6.3 10.8 %shard_map.80 = f32[2048,128]{1,0:T(8,128)S(1)} custom-call(s32[4096]{0:T(1024)S(1)} %add.108.code_ref, s32[1]{0:T(128)} %bitcast.2.me_ref, f32[16,8192]{1,0:T(8,128)S(1)} %shard_map.76.refs_0_, f32[16,8192]{1,0:T(8,128)S(1)} %shard_map.77.refs_1_, f32[16,8192]{1,0:T(8,128)S(1)} %shard_map.78.refs_2_, f32[16,8192]{1,0:T(8,128)S(1)} %shard_map.79.refs_3_), custom_call_target="tpu_custom_call" | custom-call | flops 10485760 | bytes 25165824 | tf_op jit(solution)/shard_map/pallas_call | solution.py:106
  17.2 3.0 %collective-permute-start.20 = (f32[512,128]{1,0:T(8,128)S(1)}, f32[512,128]{1,0:T(8,128)S(1)}, u32[]{:S(2)}, u32[]{:S(2)}) collective-permute-start(f32[512,128]{1,0:T(8,128)S(1)} %get-tuple-element.11), channel_id=1, source_target_pairs={{0,2},{1,3},{2,0},{3,1},{4,6},{5,7},{6,4},{7,5},{8,10},{9,11},{10,... | collective-permute-start | bytes 786440 | tf_op jit(solution)/shard_map/ppermute | solution.py:280
  20.4 6.9 %collective-permute-done.20 = f32[512,128]{1,0:T(8,128)S(1)} collective-permute-done((f32[512,128]{1,0:T(8,128)S(1)}, f32[512,128]{1,0:T(8,128)S(1)}, u32[]{:S(2)}, u32[]{:S(2)}) %collective-permute-start.20) | collective-permute-done | bytes 262176 | tf_op jit(solution)/shard_map/ppermute | solution.py:280
  27.3 4.0 %collective-permute-done.22 = f32[512,128]{1,0:T(8,128)S(1)} collective-permute-done((f32[512,128]{1,0:T(8,128)S(1)}, f32[512,128]{1,0:T(8,128)S(1)}, u32[]{:S(2)}, u32[]{:S(2)}) %collective-permute-start.22) | collective-permute-done | bytes 262176 | tf_op jit(solution)/shard_map/ppermute | solution.py:280
  35.0 2.6 %collective-permute-start = (f32[16,8192]{1,0:T(8,128)S(1)}, f32[16,8192]{1,0:T(8,128)S(1)}, u32[]{:S(2)}, u32[]{:S(2)}) collective-permute-start(f32[16,8192]{1,0:T(8,128)S(1)} %shard_map.76.refs_0_), channel_id=1, source_target_pairs={{0,16},{1,17},{2,18},{3,19},{4,20},{5,21},{6,22},{7,23},{8,24},{9,... | collective-permute-start | bytes 1572872 | tf_op jit(solution)/shard_map/ppermute | solution.py:280
  37.6 4.1 %collective-permute-done.25 = f32[128,128]{1,0:T(8,128)S(1)} collective-permute-done((f32[128,128]{1,0:T(8,128)S(1)}, f32[128,128]{1,0:T(8,128)S(1)}, u32[]{:S(2)}, u32[]{:S(2)}) %collective-permute-start.25) | collective-permute-done | bytes 65568 | tf_op jit(solution)/shard_map/ppermute | solution.py:280
  43.1 19.2 %collective-permute-done.26 = f32[64,128]{1,0:T(8,128)S(1)} collective-permute-done((f32[64,128]{1,0:T(8,128)S(1)}, f32[64,128]{1,0:T(8,128)S(1)}, u32[]{:S(2)}, u32[]{:S(2)}) %collective-permute-start.26) | collective-permute-done | bytes 32800 | tf_op jit(solution)/shard_map/ppermute | solution.py:280
  64.9 4.1 %collective-permute-start.28 = (f32[64,128]{1,0:T(8,128)}, f32[64,128]{1,0:T(8,128)S(1)}, u32[]{:S(2)}, u32[]{:S(2)}) collective-permute-start(f32[64,128]{1,0:T(8,128)} %get-tuple-element.8.refs_0_), channel_id=1, source_target_pairs={{0,8},{1,9},{2,10},{3,11},{4,12},{5,13},{6,14},{7,15},{8,0},{9,1},... | collective-permute-start | bytes 98312 | tf_op jit(solution)/shard_map/ppermute | solution.py:280
  71.1 3.8 %collective-permute-done.29.refs_3_ = f32[64,128]{1,0:T(8,128)S(1)} collective-permute-done((f32[64,128]{1,0:T(8,128)}, f32[64,128]{1,0:T(8,128)S(1)}, u32[]{:S(2)}, u32[]{:S(2)}) %collective-permute-start.29) | collective-permute-done | bytes 32800 | tf_op jit(solution)/shard_map/ppermute | solution.py:280
  86.4 3.2 %collective-permute-done.36.refs_7_ = f32[64,128]{1,0:T(8,128)S(1)} collective-permute-done((f32[64,128]{1,0:T(8,128)}, f32[64,128]{1,0:T(8,128)S(1)}, u32[]{:S(2)}, u32[]{:S(2)}) %collective-permute-start.36) | collective-permute-done | bytes 32800 | tf_op jit(solution)/shard_map/ppermute | solution.py:280
  90.2 12.6 %shard_map.83 = (f32[64,64]{1,0:T(8,128)}, f32[64,128]{1,0:T(8,128)}) custom-call(f32[64,128]{1,0:T(8,128)} %get-tuple-element.7.picked_ref, f32[64,128]{1,0:T(8,128)} %shard_map.82.refs_0_, f32[64,128]{1,0:T(8,128)} %copy-done.3, f32[64,128]{1,0:T(8,128)} %copy-done.4, f32[64,128]{1,0:T(8,128)} %copy-done.5, f32[64,128]{1,0:T(8,128)} %copy-done.6, ...), custom_call_target="tpu_custom_call" | custom-call | flops 20000000 | bytes 262144 | tf_op jit(solution)/shard_map/pallas_call | solution.py:267
  102.9 7.2 %collective-permute-done.5 = f32[16,8192]{1,0:T(8,128)} collective-permute-done((f32[16,8192]{1,0:T(8,128)S(1)}, f32[16,8192]{1,0:T(8,128)}, u32[]{:S(2)}, u32[]{:S(2)}) %collective-permute-start.5) | collective-permute-done | bytes 524320 | tf_op jit(solution)/shard_map/ppermute | solution.py:280
  115.3 6.0 %collective-permute-done.1 = f32[16,8192]{1,0:T(8,128)S(1)} collective-permute-done((f32[16,8192]{1,0:T(8,128)S(1)}, f32[16,8192]{1,0:T(8,128)S(1)}, u32[]{:S(2)}, u32[]{:S(2)}) %collective-permute-start.1) | collective-permute-done | bytes 524320 | tf_op jit(solution)/shard_map/ppermute | solution.py:280
  122.6 9.7 %collective-permute-done.6 = f32[16,8192]{1,0:T(8,128)S(1)} collective-permute-done((f32[16,8192]{1,0:T(8,128)S(1)}, f32[16,8192]{1,0:T(8,128)S(1)}, u32[]{:S(2)}, u32[]{:S(2)}) %collective-permute-start.6) | collective-permute-done | bytes 524320 | tf_op jit(solution)/shard_map/ppermute | solution.py:280
  136.1 3.7 %collective-permute-done.2 = f32[16,8192]{1,0:T(8,128)S(1)} collective-permute-done((f32[16,8192]{1,0:T(8,128)S(1)}, f32[16,8192]{1,0:T(8,128)S(1)}, u32[]{:S(2)}, u32[]{:S(2)}) %collective-permute-start.2) | collective-permute-done | bytes 524320 | tf_op jit(solution)/shard_map/ppermute | solution.py:280
  140.8 6.5 %collective-permute-done.7 = f32[16,8192]{1,0:T(8,128)S(1)} collective-permute-done((f32[16,8192]{1,0:T(8,128)S(1)}, f32[16,8192]{1,0:T(8,128)S(1)}, u32[]{:S(2)}, u32[]{:S(2)}) %collective-permute-start.7) | collective-permute-done | bytes 524320 | tf_op jit(solution)/shard_map/ppermute | solution.py:280
  148.7 2.4 %collective-permute-done.12 = f32[16,8192]{1,0:T(8,128)S(1)} collective-permute-done((f32[16,8192]{1,0:T(8,128)S(1)}, f32[16,8192]{1,0:T(8,128)S(1)}, u32[]{:S(2)}, u32[]{:S(2)}) %collective-permute-start.12) | collective-permute-done | bytes 524320 | tf_op jit(solution)/shard_map/ppermute | solution.py:280
  151.1 2.1 collective-permute-start.13
  153.2 5.3 %collective-permute-done.17 = f32[16,8192]{1,0:T(8,128)S(1)} collective-permute-done((f32[16,8192]{1,0:T(8,128)S(1)}, f32[16,8192]{1,0:T(8,128)S(1)}, u32[]{:S(2)}, u32[]{:S(2)}) %collective-permute-start.17) | collective-permute-done | bytes 524320 | tf_op jit(solution)/shard_map/ppermute | solution.py:280
  158.7 10.2 %collective-permute-done.3 = f32[16,8192]{1,0:T(8,128)S(1)} collective-permute-done((f32[16,8192]{1,0:T(8,128)S(1)}, f32[16,8192]{1,0:T(8,128)S(1)}, u32[]{:S(2)}, u32[]{:S(2)}) %collective-permute-start.3) | collective-permute-done | bytes 524320 | tf_op jit(solution)/shard_map/ppermute | solution.py:280
  169.9 5.6 %collective-permute-done.18 = f32[16,8192]{1,0:T(8,128)S(1)} collective-permute-done((f32[16,8192]{1,0:T(8,128)S(1)}, f32[16,8192]{1,0:T(8,128)S(1)}, u32[]{:S(2)}, u32[]{:S(2)}) %collective-permute-start.18) | collective-permute-done | bytes 524320 | tf_op jit(solution)/shard_map/ppermute | solution.py:280
  175.6 3.0 %collective-permute-start.19 = (f32[16,8192]{1,0:T(8,128)S(1)}, f32[16,8192]{1,0:T(8,128)S(1)}, u32[]{:S(2)}, u32[]{:S(2)}) collective-permute-start(f32[16,8192]{1,0:T(8,128)S(1)} %multiply_add_fusion.1), channel_id=1, source_target_pairs={{0,16},{1,17},{2,18},{3,19},{4,20},{5,21},{6,22},{7,23},{8,24},{9,... | collective-permute-start | bytes 1572872 | tf_op jit(solution)/shard_map/ppermute | solution.py:280
  178.8 28.4 %collective-permute-done.14 = f32[16,8192]{1,0:T(8,128)S(1)} collective-permute-done((f32[16,8192]{1,0:T(8,128)S(1)}, f32[16,8192]{1,0:T(8,128)S(1)}, u32[]{:S(2)}, u32[]{:S(2)}) %collective-permute-start.14) | collective-permute-done | bytes 524320 | tf_op jit(solution)/shard_map/ppermute | solution.py:280
  207.3 10.7 %collective-permute-done.19 = f32[16,8192]{1,0:T(8,128)S(1)} collective-permute-done((f32[16,8192]{1,0:T(8,128)S(1)}, f32[16,8192]{1,0:T(8,128)S(1)}, u32[]{:S(2)}, u32[]{:S(2)}) %collective-permute-start.19) | collective-permute-done | bytes 524320 | tf_op jit(solution)/shard_map/ppermute | solution.py:280
  (117 shorter events, 43.5 us)
Async XLA Ops:
  17.2 10.2 %collective-permute-start.20 = (f32[512,128]{1,0:T(8,128)S(1)}, f32[512,128]{1,0:T(8,128)S(1)}, u32[]{:S(2)}, u32[]{:S(2)}) collective-permute-start(f32[512,128]{1,0:T(8,128)S(1)} %get-tuple-element.11), channel_id=1, source_target_pairs={{0,2},{1,3},{2,0},{3,1},{4,6},{5,7},{6,4},{7,5},{8,10},{9,11},{10,... | collective-permute-start | bytes 786440 | tf_op jit(solution)/shard_map/ppermute | solution.py:280
  20.2 7.1 %collective-permute-start.21 = (f32[512,128]{1,0:T(8,128)S(1)}, f32[512,128]{1,0:T(8,128)S(1)}, u32[]{:S(2)}, u32[]{:S(2)}) collective-permute-start(f32[512,128]{1,0:T(8,128)S(1)} %get-tuple-element.13), channel_id=1, source_target_pairs={{0,1},{1,0},{2,3},{3,2},{4,5},{5,4},{6,7},{7,6},{8,9},{9,8},{10,11... | collective-permute-start | bytes 786440 | tf_op jit(solution)/shard_map/ppermute | solution.py:280
  20.2 11.2 %collective-permute-start.22 = (f32[512,128]{1,0:T(8,128)S(1)}, f32[512,128]{1,0:T(8,128)S(1)}, u32[]{:S(2)}, u32[]{:S(2)}) collective-permute-start(f32[512,128]{1,0:T(8,128)S(1)} %get-tuple-element.12), channel_id=1, source_target_pairs={{0,3},{1,2},{2,1},{3,0},{4,7},{5,6},{6,5},{7,4},{8,11},{9,10},{10,... | collective-permute-start | bytes 786440 | tf_op jit(solution)/shard_map/ppermute | solution.py:280
  35.0 67.7 %collective-permute-start = (f32[16,8192]{1,0:T(8,128)S(1)}, f32[16,8192]{1,0:T(8,128)S(1)}, u32[]{:S(2)}, u32[]{:S(2)}) collective-permute-start(f32[16,8192]{1,0:T(8,128)S(1)} %shard_map.76.refs_0_), channel_id=1, source_target_pairs={{0,16},{1,17},{2,18},{3,19},{4,20},{5,21},{6,22},{7,23},{8,24},{9,... | collective-permute-start | bytes 1572872 | tf_op jit(solution)/shard_map/ppermute | solution.py:280
  41.7 20.6 %collective-permute-start.26 = (f32[64,128]{1,0:T(8,128)S(1)}, f32[64,128]{1,0:T(8,128)S(1)}, u32[]{:S(2)}, u32[]{:S(2)}) collective-permute-start(f32[64,128]{1,0:T(8,128)S(1)} %slice.49), channel_id=1, source_target_pairs={{0,16},{1,17},{2,18},{3,19},{4,20},{5,21},{6,22},{7,23},{8,24},{9,... | collective-permute-start | bytes 98312 | tf_op jit(solution)/shard_map/ppermute | solution.py:280
  85.1 25.0 %collective-permute-start.5 = (f32[16,8192]{1,0:T(8,128)S(1)}, f32[16,8192]{1,0:T(8,128)}, u32[]{:S(2)}, u32[]{:S(2)}) collective-permute-start(f32[16,8192]{1,0:T(8,128)S(1)} %shard_map.77.refs_1_), channel_id=1, source_target_pairs={{0,16},{1,17},{2,18},{3,19},{4,20},{5,21},{6,22},{7,23},{8,24},{9,... | collective-permute-start | bytes 1572872 | tf_op jit(solution)/shard_map/ppermute | solution.py:280
  85.2 26.0 %collective-permute-start.10 = (f32[16,8192]{1,0:T(8,128)S(1)}, f32[16,8192]{1,0:T(8,128)}, u32[]{:S(2)}, u32[]{:S(2)}) collective-permute-start(f32[16,8192]{1,0:T(8,128)S(1)} %shard_map.78.refs_2_), channel_id=1, source_target_pairs={{0,1},{1,0},{2,3},{3,2},{4,5},{5,4},{6,7},{7,6},{8,9},{9,8},{10,11... | collective-permute-start | bytes 1572872 | tf_op jit(solution)/shard_map/ppermute | solution.py:280
  86.3 27.4 %collective-permute-start.15 = (f32[16,8192]{1,0:T(8,128)S(1)}, f32[16,8192]{1,0:T(8,128)S(1)}, u32[]{:S(2)}, u32[]{:S(2)}) collective-permute-start(f32[16,8192]{1,0:T(8,128)S(1)} %shard_map.79.refs_3_), channel_id=1, source_target_pairs={{0,1},{1,0},{2,3},{3,2},{4,5},{5,4},{6,7},{7,6},{8,9},{9,8},{10,11... | collective-permute-start | bytes 1572872 | tf_op jit(solution)/shard_map/ppermute | solution.py:280
  102.8 18.4 %collective-permute-start.1 = (f32[16,8192]{1,0:T(8,128)S(1)}, f32[16,8192]{1,0:T(8,128)S(1)}, u32[]{:S(2)}, u32[]{:S(2)}) collective-permute-start(f32[16,8192]{1,0:T(8,128)S(1)} %multiply_add_fusion.19), channel_id=1, source_target_pairs={{0,8},{1,9},{2,10},{3,11},{4,12},{5,13},{6,14},{7,15},{8,0},{9,1},... | collective-permute-start | bytes 1572872 | tf_op jit(solution)/shard_map/ppermute | solution.py:280
  111.2 21.2 %collective-permute-start.6 = (f32[16,8192]{1,0:T(8,128)S(1)}, f32[16,8192]{1,0:T(8,128)S(1)}, u32[]{:S(2)}, u32[]{:S(2)}) collective-permute-start(f32[16,8192]{1,0:T(8,128)S(1)} %multiply_add_fusion.14), channel_id=1, source_target_pairs={{0,8},{1,9},{2,10},{3,11},{4,12},{5,13},{6,14},{7,15},{8,0},{9,1},... | collective-permute-start | bytes 1572872 | tf_op jit(solution)/shard_map/ppermute | solution.py:280
  112.4 21.3 %collective-permute-start.11 = (f32[16,8192]{1,0:T(8,128)S(1)}, f32[16,8192]{1,0:T(8,128)S(1)}, u32[]{:S(2)}, u32[]{:S(2)}) collective-permute-start(f32[16,8192]{1,0:T(8,128)S(1)} %multiply_add_fusion.9), channel_id=1, source_target_pairs={{0,2},{1,3},{2,0},{3,1},{4,6},{5,7},{6,4},{7,5},{8,10},{9,11},{10,... | collective-permute-start | bytes 1572872 | tf_op jit(solution)/shard_map/ppermute | solution.py:280
  113.7 21.7 %collective-permute-start.16 = (f32[16,8192]{1,0:T(8,128)S(1)}, f32[16,8192]{1,0:T(8,128)S(1)}, u32[]{:S(2)}, u32[]{:S(2)}) collective-permute-start(f32[16,8192]{1,0:T(8,128)S(1)} %multiply_add_fusion.4), channel_id=1, source_target_pairs={{0,4},{1,5},{2,6},{3,7},{4,0},{5,1},{6,2},{7,3},{8,12},{9,13},{10,... | collective-permute-start | bytes 1572872 | tf_op jit(solution)/shard_map/ppermute | solution.py:280
  121.3 18.5 %collective-permute-start.2 = (f32[16,8192]{1,0:T(8,128)S(1)}, f32[16,8192]{1,0:T(8,128)S(1)}, u32[]{:S(2)}, u32[]{:S(2)}) collective-permute-start(f32[16,8192]{1,0:T(8,128)S(1)} %multiply_add_fusion.18), channel_id=1, source_target_pairs={{0,4},{1,5},{2,6},{3,7},{4,0},{5,1},{6,2},{7,3},{8,12},{9,13},{10,... | collective-permute-start | bytes 1572872 | tf_op jit(solution)/shard_map/ppermute | solution.py:280
  132.4 14.8 %collective-permute-start.7 = (f32[16,8192]{1,0:T(8,128)S(1)}, f32[16,8192]{1,0:T(8,128)S(1)}, u32[]{:S(2)}, u32[]{:S(2)}) collective-permute-start(f32[16,8192]{1,0:T(8,128)S(1)} %multiply_add_fusion.13), channel_id=1, source_target_pairs={{0,2},{1,3},{2,0},{3,1},{4,6},{5,7},{6,4},{7,5},{8,10},{9,11},{10,... | collective-permute-start | bytes 1572872 | tf_op jit(solution)/shard_map/ppermute | solution.py:280
  133.8 17.3 %collective-permute-start.12 = (f32[16,8192]{1,0:T(8,128)S(1)}, f32[16,8192]{1,0:T(8,128)S(1)}, u32[]{:S(2)}, u32[]{:S(2)}) collective-permute-start(f32[16,8192]{1,0:T(8,128)S(1)} %multiply_add_fusion.8), channel_id=1, source_target_pairs={{0,4},{1,5},{2,6},{3,7},{4,0},{5,1},{6,2},{7,3},{8,12},{9,13},{10,... | collective-permute-start | bytes 1572872 | tf_op jit(solution)/shard_map/ppermute | solution.py:280
  135.4 23.1 %collective-permute-start.17 = (f32[16,8192]{1,0:T(8,128)S(1)}, f32[16,8192]{1,0:T(8,128)S(1)}, u32[]{:S(2)}, u32[]{:S(2)}) collective-permute-start(f32[16,8192]{1,0:T(8,128)S(1)} %multiply_add_fusion.3), channel_id=1, source_target_pairs={{0,2},{1,3},{2,0},{3,1},{4,6},{5,7},{6,4},{7,5},{8,10},{9,11},{10,... | collective-permute-start | bytes 1572872 | tf_op jit(solution)/shard_map/ppermute | solution.py:280
  139.9 28.9 %collective-permute-start.3 = (f32[16,8192]{1,0:T(8,128)S(1)}, f32[16,8192]{1,0:T(8,128)S(1)}, u32[]{:S(2)}, u32[]{:S(2)}) collective-permute-start(f32[16,8192]{1,0:T(8,128)S(1)} %multiply_add_fusion.17), channel_id=1, source_target_pairs={{0,2},{1,3},{2,0},{3,1},{4,6},{5,7},{6,4},{7,5},{8,10},{9,11},{10,... | collective-permute-start | bytes 1572872 | tf_op jit(solution)/shard_map/ppermute | solution.py:280
  147.4 21.6 %collective-permute-start.8 = (f32[16,8192]{1,0:T(8,128)S(1)}, f32[16,8192]{1,0:T(8,128)S(1)}, u32[]{:S(2)}, u32[]{:S(2)}) collective-permute-start(f32[16,8192]{1,0:T(8,128)S(1)} %multiply_add_fusion.12), channel_id=1, source_target_pairs={{0,4},{1,5},{2,6},{3,7},{4,0},{5,1},{6,2},{7,3},{8,12},{9,13},{10,... | collective-permute-start | bytes 1572872 | tf_op jit(solution)/shard_map/ppermute | solution.py:280
  151.1 18.5 %collective-permute-start.13 = (f32[16,8192]{1,0:T(8,128)S(1)}, f32[16,8192]{1,0:T(8,128)S(1)}, u32[]{:S(2)}, u32[]{:S(2)}) collective-permute-start(f32[16,8192]{1,0:T(8,128)S(1)} %multiply_add_fusion.7), channel_id=1, source_target_pairs={{0,8},{1,9},{2,10},{3,11},{4,12},{5,13},{6,14},{7,15},{8,0},{9,1},... | collective-permute-start | bytes 1572872 | tf_op jit(solution)/shard_map/ppermute | solution.py:280
  158.6 16.9 %collective-permute-start.18 = (f32[16,8192]{1,0:T(8,128)S(1)}, f32[16,8192]{1,0:T(8,128)S(1)}, u32[]{:S(2)}, u32[]{:S(2)}) collective-permute-start(f32[16,8192]{1,0:T(8,128)S(1)} %multiply_add_fusion.2), channel_id=1, source_target_pairs={{0,8},{1,9},{2,10},{3,11},{4,12},{5,13},{6,14},{7,15},{8,0},{9,1},... | collective-permute-start | bytes 1572872 | tf_op jit(solution)/shard_map/ppermute | solution.py:280
  168.9 9.7 %collective-permute-start.4 = (f32[16,8192]{1,0:T(8,128)S(1)}, f32[16,8192]{1,0:T(8,128)S(1)}, u32[]{:S(2)}, u32[]{:S(2)}) collective-permute-start(f32[16,8192]{1,0:T(8,128)S(1)} %multiply_add_fusion.16), channel_id=1, source_target_pairs={{0,1},{1,0},{2,3},{3,2},{4,5},{5,4},{6,7},{7,6},{8,9},{9,8},{10,11... | collective-permute-start | bytes 1572872 | tf_op jit(solution)/shard_map/ppermute | solution.py:280
  169.0 9.7 %collective-permute-start.9 = (f32[16,8192]{1,0:T(8,128)S(1)}, f32[16,8192]{1,0:T(8,128)S(1)}, u32[]{:S(2)}, u32[]{:S(2)}) collective-permute-start(f32[16,8192]{1,0:T(8,128)S(1)} %multiply_add_fusion.11), channel_id=1, source_target_pairs={{0,1},{1,0},{2,3},{3,2},{4,5},{5,4},{6,7},{7,6},{8,9},{9,8},{10,11... | collective-permute-start | bytes 1572872 | tf_op jit(solution)/shard_map/ppermute | solution.py:280
  169.7 37.5 %collective-permute-start.14 = (f32[16,8192]{1,0:T(8,128)S(1)}, f32[16,8192]{1,0:T(8,128)S(1)}, u32[]{:S(2)}, u32[]{:S(2)}) collective-permute-start(f32[16,8192]{1,0:T(8,128)S(1)} %multiply_add_fusion.6), channel_id=1, source_target_pairs={{0,16},{1,17},{2,18},{3,19},{4,20},{5,21},{6,22},{7,23},{8,24},{9,... | collective-permute-start | bytes 1572872 | tf_op jit(solution)/shard_map/ppermute | solution.py:280
  175.6 42.4 %collective-permute-start.19 = (f32[16,8192]{1,0:T(8,128)S(1)}, f32[16,8192]{1,0:T(8,128)S(1)}, u32[]{:S(2)}, u32[]{:S(2)}) collective-permute-start(f32[16,8192]{1,0:T(8,128)S(1)} %multiply_add_fusion.1), channel_id=1, source_target_pairs={{0,16},{1,17},{2,18},{3,19},{4,20},{5,21},{6,22},{7,23},{8,24},{9,... | collective-permute-start | bytes 1572872 | tf_op jit(solution)/shard_map/ppermute | solution.py:280
  (28 other events, 112.3 us)

commit v2 on v1

--- a/solution.py
+++ b/solution.py
@@ -20,6 +20,10 @@
     while table.shape[0] < order_size:
         table = np.block([[table, table], [table, -table]])
     return table
+
+
+def in_hbm(value):
+    return pltpu.with_memory_space_constraint(value, pltpu.HBM)
 
 
 def mix_kernel(scale, panel_ref, signs_ref, table_ref, out_ref):
@@ -46,43 +50,106 @@
                 left, right = blocks[a], blocks[a + span]
                 blocks[a], blocks[a + span] = left + right, left - right
         span *= 2
-    for a in range(inner):
-        out_ref[:, a * LANES : (a + 1) * LANES] = blocks[a]
-
-
-def local_mix(panel, signs_row, table, scale, first, count):
-    rows = panel.shape[1]
+    peers, _, width = out_ref.shape
+    step = min(width, LANES)
+    for start in range(0, rows, step):
+        block = blocks[start // LANES][:, start % LANES : start % LANES + step]
+        out_ref[start // width, :, start % width : start % width + step] = block
+
+
+def local_mix(panel, signs_row, table, scale, peers):
+    cols, rows = panel.shape
+    width = rows // peers
     return pl.pallas_call(
         functools.partial(mix_kernel, scale),
-        grid=(count // GROUP,),
+        grid=(cols // GROUP,),
         in_specs=[
-            pl.BlockSpec((GROUP, rows), lambda i: (first // GROUP + i, 0)),
+            pl.BlockSpec((GROUP, rows), lambda i: (i, 0)),
             pl.BlockSpec((1, rows), lambda i: (0, 0)),
             pl.BlockSpec((LANES, LANES), lambda i: (0, 0)),
         ],
-        out_specs=pl.BlockSpec((GROUP, rows), lambda i: (i, 0)),
-        out_shape=jax.ShapeDtypeStruct((count, rows), jnp.float32),
+        out_specs=pl.BlockSpec((peers, GROUP, width), lambda i: (0, i, 0)),
+        out_shape=pltpu.HBM((peers, cols, width), jnp.float32),
         compiler_params=pltpu.CompilerParams(vmem_limit_bytes=32 << 20),
-        cost_estimate=pl.CostEstimate(
-            flops=count * rows * 800, bytes_accessed=count * rows * 8, transcendentals=0
-        ),
-    )(panel, signs_row, table)
-
-
-def terms_kernel(bits, half, code_ref, me_ref, *refs):
-    chunk_refs, out_ref, table_ref = refs[:-2], refs[-2], refs[-1]
-    rows = chunk_refs[0].shape[1]
+    )(in_hbm(panel), signs_row, table)
+
+
+def across_kernel(in_ref, out_ref):
+    peers = in_ref.shape[0]
+    step = min(in_ref.shape[2], LANES)
+    for lane in range(0, in_ref.shape[2], step):
+        blocks = [in_ref[p, :, lane : lane + step] for p in range(peers)]
+        span = 1
+        while span < peers:
+            for p in range(peers):
+                if p & span == 0:
+                    left, right = blocks[p], blocks[p + span]
+                    blocks[p], blocks[p + span] = left + right, left - right
+            span *= 2
+        for p in range(peers):
+            out_ref[p, :, lane : lane + step] = blocks[p]
+
+
+def mix_across(received):
+    peers, cols, width = received.shape
+    spec = pl.BlockSpec((peers, GROUP, width), lambda i: (0, i, 0))
+    return pl.pallas_call(
+        across_kernel,
+        grid=(cols // GROUP,),
+        in_specs=[spec],
+        out_specs=spec,
+        out_shape=pltpu.HBM(received.shape, jnp.float32),
+        compiler_params=pltpu.CompilerParams(vmem_limit_bytes=32 << 20),
+    )(in_hbm(received))
+
+
+def lay_out_kernel(in_ref, out_ref):
+    peers, _, width = in_ref.shape
+    for p in range(peers):
+        out_ref[:, p * width : (p + 1) * width] = in_ref[p]
+
+
+def lay_out(received):
+    peers, cols, width = received.shape
+    return pl.pallas_call(
+        lay_out_kernel,
+        grid=(cols // GROUP,),
+        in_specs=[pl.BlockSpec((peers, GROUP, width), lambda i: (0, i, 0))],
+        out_specs=pl.BlockSpec((GROUP, peers * width), lambda i: (i, 0)),
+        out_shape=jax.ShapeDtypeStruct((cols, peers * width), jnp.float32),
+        compiler_params=pltpu.CompilerParams(vmem_limit_bytes=32 << 20),
+    )(in_hbm(received))
+
+
+def terms_kernel(bits, half, code_ref, me_ref, far_ref, out_ref, mix_ref, table_ref, done_sem):
+    peers, _, width = mix_ref.shape
+    pieces = [
+        pltpu.make_async_copy(far_ref.at[part], mix_ref.at[part], done_sem.at[number])
+        for number, part in enumerate([pl.ds(0, peers // 2), pl.ds(peers // 2, peers // 2)])
+    ]
+    for piece in pieces:
+        piece.start()
+    rows = peers * width
     me = me_ref[0]
 
-    def transpose_block(a, carry):
-        start = pl.multiple_of(a * LANES, LANES)
-        tile = jnp.concatenate([ref[:, pl.ds(start, LANES)] for ref in chunk_refs], axis=0)
-        turned = jnp.concatenate([tile, tile], axis=0).T
-        table_ref[pl.ds(start, LANES), :] = turned
-        table_ref[pl.ds(rows + start, LANES), :] = -turned
+    span = max(1, LANES // width)
+
+    def transpose_block(number, carry):
+        p = number * span
+        for lane in range(0, max(width, LANES), LANES):
+            start = pl.multiple_of(p * width + lane, LANES)
+            tile = jnp.concatenate(
+                [mix_ref[p + i, :, lane : lane + min(width, LANES)] for i in range(span)], axis=1
+            )
+            turned = jnp.concatenate([tile, tile], axis=0).T
+            table_ref[pl.ds(start, LANES), :] = turned
+            table_ref[pl.ds(rows + start, LANES), :] = -turned
         return carry
 
-    lax.fori_loop(0, rows // LANES, transpose_block, 0)
+    for number, piece in enumerate(pieces):
+        piece.wait()
+        count = peers // 2 // span
+        lax.fori_loop(number * count, (number + 1) * count, transpose_block, 0)
     first_half = lax.broadcasted_iota(jnp.int32, (1, LANES), 1) < LANES // 2
 
     def gather_block(r, carry):
@@ -100,21 +167,25 @@
     lax.fori_loop(0, 1 << bits, gather_block, 0)
 
 
-def sampled_terms(chunks, code, me, bits, half):
-    rows = chunks[0].shape[1]
+def sampled_terms(mix, code, me, bits, half):
+    rows = mix.shape[0] * mix.shape[2]
     count = half << bits
     return pl.pallas_call(
         functools.partial(terms_kernel, bits, half),
         in_specs=[pl.BlockSpec(memory_space=pltpu.SMEM)] * 2
-        + [pl.BlockSpec(memory_space=pltpu.VMEM)] * len(chunks),
+        + [pl.BlockSpec(memory_space=pltpu.HBM)],
         out_specs=pl.BlockSpec(memory_space=pltpu.VMEM),
         out_shape=jax.ShapeDtypeStruct((count, LANES), jnp.float32),
-        scratch_shapes=[pltpu.VMEM((2 * rows, LANES), jnp.float32)],
+        scratch_shapes=[
+            pltpu.VMEM(mix.shape, jnp.float32),
+            pltpu.VMEM((2 * rows, LANES), jnp.float32),
+            pltpu.SemaphoreType.DMA((2,)),
+        ],
         compiler_params=pltpu.CompilerParams(vmem_limit_bytes=40 << 20),
         cost_estimate=pl.CostEstimate(
             flops=count * LANES * 40, bytes_accessed=24 << 20, transcendentals=0
         ),
-    )(code, me, *chunks)
+    )(code, me, in_hbm(mix))
 
 
 def two_sum(a, b):
@@ -280,8 +351,10 @@
     return lax.ppermute(value, AXES, [(i, i ^ mask) for i in range(device_count)])
 
 
-def in_groups(masks, size):
-    return [masks[i : i + size] for i in range(0, len(masks), size)]
+def in_groups(masks, size=2):
+    odd = len(masks) % size
+    groups = [masks[:odd]] if odd else []
+    return groups + [masks[i : i + size] for i in range(odd, len(masks), size)]
 
 
 def combined(masks, q):
@@ -306,46 +379,27 @@
     signs_row = signs.reshape(1, rows)
     scale = 1.0 / math.sqrt(rows * device_count)
 
-    parts = 4
-    width = cols // parts
-    chunks = [
-        local_mix(panel, signs_row, table, scale, part * width, width) for part in range(parts)
-    ]
-
-    far = masks[::-1]
-    swapped = list(masks)
-    if bits > 2:
-        swapped[1], swapped[2] = swapped[2], swapped[1]
-    orders = [far, swapped[::-1], masks, swapped]
-
-    def own_sign(mask):
-        return jnp.where((me & mask) == 0, jnp.float32(1.0), jnp.float32(-1.0))
-
-    done = []
-    for chunk, order in zip(chunks, orders):
-        value = chunk
-        for mask in order:
-            other = xor_permute(value, mask, device_count)
-            value = other + own_sign(mask) * value
-        done.append(value)
-    mixed = jnp.concatenate(done, axis=0)
+    mix = local_mix(panel, signs_row, table, scale, device_count)
+
+    def swap(value):
+        return lax.all_to_all(value, AXES, split_axis=0, concat_axis=0, tiled=True)
+
+    mixed = lay_out(swap(mix_across(swap(mix))))
 
     common = me & sample_device[:, 0]
     odd = lax.population_count(common) & 1
     code = sample_offset + odd * rows
-    total = sampled_terms(chunks, code, me.reshape(1), bits, half)
-    for group in in_groups(masks, 2):
+    total = sampled_terms(mix, code, me.reshape(1), bits, half)
+    for group in in_groups(masks):
         block = total.shape[0] >> len(group)
         mine = total[:block]
         for q in range(1, 1 << len(group)):
             mask = combined(group[::-1], q)
-            mine = mine + xor_permute(total[q * block : (q + 1) * block], mask, device_count)
+            sent = total[q * block : (q + 1) * block]
+            mine = mine + xor_permute(sent, mask, device_count)
         total = mine
-
     picked, gram = own_gram(total, cols, per_device, 1.0 / math.sqrt(samples))
-    groups = in_groups(far, 2)
-    if len(groups) > 1 and len(groups[-1]) == 1:
-        groups = groups[:-2] + [groups[-2] + groups[-1]]
+    groups = in_groups(masks)[::-1]
     for number, group in enumerate(groups):
         received = [gram] + [
             xor_permute(gram, combined(group, q), device_count) for q in range(1, 1 << len(group))

time: 220 us -> 171 us (0.78)
  waiting for transfers between devices: 142 us -> 43.4 us
  blocking collectives: 0 us -> 56.1 us
  starting transfers between devices: 37.7 us -> 19.9 us
  Pallas kernels: 29.3 us -> 44.5 us
  other arithmetic: 5.58 us -> 0.76 us
    ppermute x37 -> x14, waiting for transfers between devices: 142 us -> 43.4 us  [xor_permute(): lax.ppermute(value, AXES, [(i, i ^ mask) for i in range(device_count)])]
    all_to_all x0 -> x1, blocking collectives: none -> 56.1 us  [swap(): return lax.all_to_all(value, AXES, split_axis=0, concat_axis=0, tiled=True)]
    ppermute x37 -> x14, starting transfers between devices: 37.7 us -> 16.2 us  [xor_permute(): lax.ppermute(value, AXES, [(i, i ^ mask) for i in range(device_count)])]
    pallas_call x4 -> x3, Pallas kernels: 2.41 us -> 18.1 us  [the longest x1 6.63 us: local_mix(): pl.pallas_call(functools.partial(mix_kernel, scale), grid=(cols // GROUP,...]
    all_to_all x0 -> x1, starting transfers between devices: none -> 3.67 us  [swap(): return lax.all_to_all(value, AXES, split_axis=0, concat_axis=0, tiled=True)]
    add x23 -> x3, other arithmetic: 4.08 us -> 0.73 us  [local(): mine = mine + xor_permute(sent, mask, device_count)]
    unnamed x30 -> x24, local copies, waits for them, and re-layouts: 4.3 us -> 4.68 us
  transfers between devices with their start and end apart: 37 -> 15, of which waited for: 23 -> 10; matrix products, arithmetic and copies ran while one was open for 2% -> 0% of each run, Pallas kernels for 7% -> 16%
where the time goes in v2:
time: 171 us; the launch traced here: 170 us
  blocking collectives  56.1 us (33%)
  Pallas kernels  44.5 us (26%)
  waiting for transfers between devices  43.4 us (25%)
  starting transfers between devices  19.9 us (12%)
  local copies, waits for them, and re-layouts  4.75 us (3%)
    all_to_all x1, blocking collectives, swap(): return lax.all_to_all(value, AXES, split_axis=0, concat_axis=0, tiled=True)  56.1 us
    ppermute x14, waiting for transfers between devices, xor_permute(): lax.ppermute(value, AXES, [(i, i ^ mask) for i in range(device_count)])  43.4 us
    ppermute x14, starting transfers between devices, xor_permute(): lax.ppermute(value, AXES, [(i, i ^ mask) for i in range(device_count)])  16.2 us
    pallas_call x1, Pallas kernels, factor_and_solve(): pl.pallas_call(factor_kernel, out_shape=(jax.ShapeDtypeStruct((cols, cols...  12.5 us
    pallas_call x1, Pallas kernels, sampled_terms(): pl.pallas_call(functools.partial(terms_kernel, bits, half), in_specs=[pl....  8.81 us
    pallas_call x1, Pallas kernels, local_mix(): pl.pallas_call(functools.partial(mix_kernel, scale), grid=(cols // GROUP,...  6.63 us
    pallas_call x1, Pallas kernels, mix_across(): pl.pallas_call(across_kernel, grid=(cols // GROUP,), in_specs=[spec], out...  5.84 us
    pallas_call x1, Pallas kernels, lay_out(): pl.pallas_call(lay_out_kernel, grid=(cols // GROUP,), in_specs=[pl.BlockS...  5.63 us
  transfers between devices with their start and end apart: 15, of which 10 were waited for; matrix products, arithmetic and copies ran while one was open for 0% of the time, Pallas kernels for 16%

profile of v2, /device:TPU:0, one launch (start us, length us, event | category | flops | bytes accessed | tf_op | source)
XLA Modules:
  0.0 170.2 jit_solution(101515030974325425)
XLA Ops:
  2.1 6.6 %shard_map.76.far_ref = f32[32,64,256]{2,1,0:T(8,128)} custom-call(f32[64,8192]{1,0:T(8,128)} %panel_ref.1, s32[1,8192]{1,0:T(1,128)S(1)} %bitcast.3, bf16[128,128]{1,0:T(8,128)(2,1)S(1)} %copy-done.1), custom_call_target="tpu_custom_call" | custom-call | tf_op jit(solution)/shard_map/pallas_call | solution.py:63
  8.8 56.1 %all_to_all.10.in_ref = f32[32,64,256]{2,1,0:T(8,128)} all-to-all(f32[32,64,256]{2,1,0:T(8,128)} %shard_map.76.far_ref), channel_id=1, replica_groups=mesh['rows'=8,'sk'=4] {'rows','sk'}, dimensions={0} | all-to-all | bytes 4194304 | tf_op jit(solution)/shard_map/all_to_all | solution.py:385
  64.9 5.8 %shard_map.77 = f32[32,64,256]{2,1,0:T(8,128)} custom-call(f32[32,64,256]{2,1,0:T(8,128)} %all_to_all.10.in_ref), custom_call_target="tpu_custom_call" | custom-call | tf_op jit(solution)/shard_map/pallas_call | solution.py:96
  70.7 3.7 %all-to-all-start.1 = ((f32[32,64,256]{2,1,0:T(8,128)}), f32[32,64,256]{2,1,0:T(8,128)S(1)}, u32[]{:S(2)}, u32[]{:S(2)}) async-start(f32[32,64,256]{2,1,0:T(8,128)} %shard_map.77), calls=%async_computation.1 | async-start | bytes 4194304 | tf_op jit(solution)/shard_map/all_to_all | solution.py:385
  74.5 8.8 %shard_map.79 = f32[2048,128]{1,0:T(8,128)S(1)} custom-call(s32[4096]{0:T(1024)S(1)} %add.28.code_ref, s32[1]{0:T(128)} %bitcast.2.me_ref, f32[32,64,256]{2,1,0:T(8,128)} %shard_map.76.far_ref), custom_call_target="tpu_custom_call" | custom-call | flops 10485760 | bytes 25165824 | tf_op jit(solution)/shard_map/pallas_call | solution.py:173
  83.7 1.7 collective-permute-done
  85.4 1.8 %collective-permute-start.1 = (f32[256,128]{1,0:T(8,128)S(1)}, f32[256,128]{1,0:T(8,128)S(1)}, u32[]{:S(2)}, u32[]{:S(2)}) collective-permute-start(f32[256,128]{1,0:T(8,128)S(1)} %get-tuple-element.11), channel_id=1, source_target_pairs={{0,4},{1,5},{2,6},{3,7},{4,0},{5,1},{6,2},{7,3},{8,12},{9,13},{10,... | collective-permute-start | bytes 393224 | tf_op jit(solution)/shard_map/ppermute | solution.py:351
  87.3 1.5 collective-permute-start.2
  89.0 6.7 %collective-permute-done.1 = f32[256,128]{1,0:T(8,128)S(1)} collective-permute-done((f32[256,128]{1,0:T(8,128)S(1)}, f32[256,128]{1,0:T(8,128)S(1)}, u32[]{:S(2)}, u32[]{:S(2)}) %collective-permute-start.1) | collective-permute-done | bytes 131104 | tf_op jit(solution)/shard_map/ppermute | solution.py:351
  95.7 7.9 %collective-permute-done.3 = f32[256,128]{1,0:T(8,128)S(1)} collective-permute-done((f32[256,128]{1,0:T(8,128)S(1)}, f32[256,128]{1,0:T(8,128)S(1)}, u32[]{:S(2)}, u32[]{:S(2)}) %collective-permute-start.3) | collective-permute-done | bytes 131104 | tf_op jit(solution)/shard_map/ppermute | solution.py:351
  103.7 1.7 collective-permute-start.5
  105.4 2.7 %collective-permute-start.6 = (f32[64,128]{1,0:T(8,128)S(1)}, f32[64,128]{1,0:T(8,128)S(1)}, u32[]{:S(2)}, u32[]{:S(2)}) collective-permute-start(f32[64,128]{1,0:T(8,128)S(1)} %get-tuple-element.15), channel_id=1, source_target_pairs={{0,24},{1,25},{2,26},{3,27},{4,28},{5,29},{6,30},{7,31},{8,16},{9,... | collective-permute-start | bytes 98312 | tf_op jit(solution)/shard_map/ppermute | solution.py:351
  108.1 17.5 %collective-permute-done.4 = f32[64,128]{1,0:T(8,128)S(1)} collective-permute-done((f32[64,128]{1,0:T(8,128)S(1)}, f32[64,128]{1,0:T(8,128)S(1)}, u32[]{:S(2)}, u32[]{:S(2)}) %collective-permute-start.4) | collective-permute-done | bytes 32800 | tf_op jit(solution)/shard_map/ppermute | solution.py:351
  126.3 1.9 %shard_map.80 = (f32[64,128]{1,0:T(8,128)}, f32[64,128]{1,0:T(8,128)}) custom-call(f32[64,128]{1,0:T(8,128)} %fusion.3.terms_ref), custom_call_target="tpu_custom_call" | custom-call | tf_op jit(solution)/shard_map/pallas_call | solution.py:250
  130.0 2.6 %collective-permute-start.9 = (f32[64,128]{1,0:T(8,128)}, f32[64,128]{1,0:T(8,128)S(1)}, u32[]{:S(2)}, u32[]{:S(2)}) collective-permute-start(f32[64,128]{1,0:T(8,128)} %get-tuple-element.8.refs_0_), channel_id=1, source_target_pairs={{0,24},{1,25},{2,26},{3,27},{4,28},{5,29},{6,30},{7,31},{8,16},{9,... | collective-permute-start | bytes 98312 | tf_op jit(solution)/shard_map/ppermute | solution.py:351
  132.6 2.2 %collective-permute-done.8.refs_2_ = f32[64,128]{1,0:T(8,128)S(1)} collective-permute-done((f32[64,128]{1,0:T(8,128)}, f32[64,128]{1,0:T(8,128)S(1)}, u32[]{:S(2)}, u32[]{:S(2)}) %collective-permute-start.8) | collective-permute-done | bytes 32800 | tf_op jit(solution)/shard_map/ppermute | solution.py:351
  136.5 1.6 shard_map.81.refs_0_
  138.1 1.7 %collective-permute-start.10 = (f32[64,128]{1,0:T(8,128)}, f32[64,128]{1,0:T(8,128)S(1)}, u32[]{:S(2)}, u32[]{:S(2)}) collective-permute-start(f32[64,128]{1,0:T(8,128)} %shard_map.81.refs_0_), channel_id=1, source_target_pairs={{0,2},{1,3},{2,0},{3,1},{4,6},{5,7},{6,4},{7,5},{8,10},{9,11},{10,... | collective-permute-start | bytes 98312 | tf_op jit(solution)/shard_map/ppermute | solution.py:351
  139.8 1.7 collective-permute-start.11
  142.2 1.7 %collective-permute-done.11.refs_2_ = f32[64,128]{1,0:T(8,128)S(1)} collective-permute-done((f32[64,128]{1,0:T(8,128)}, f32[64,128]{1,0:T(8,128)S(1)}, u32[]{:S(2)}, u32[]{:S(2)}) %collective-permute-start.11) | collective-permute-done | bytes 32800 | tf_op jit(solution)/shard_map/ppermute | solution.py:351
  143.9 2.6 %collective-permute-done.12.refs_3_ = f32[64,128]{1,0:T(8,128)S(1)} collective-permute-done((f32[64,128]{1,0:T(8,128)}, f32[64,128]{1,0:T(8,128)S(1)}, u32[]{:S(2)}, u32[]{:S(2)}) %collective-permute-start.12) | collective-permute-done | bytes 32800 | tf_op jit(solution)/shard_map/ppermute | solution.py:351
  147.1 1.6 shard_map.82.refs_0_
  150.7 12.5 %shard_map.83 = (f32[64,64]{1,0:T(8,128)}, f32[64,128]{1,0:T(8,128)}) custom-call(f32[64,128]{1,0:T(8,128)} %get-tuple-element.7.picked_ref, f32[64,128]{1,0:T(8,128)} %shard_map.82.refs_0_, f32[64,128]{1,0:T(8,128)} %copy-done.9), custom_call_target="tpu_custom_call" | custom-call | flops 20000000 | bytes 262144 | tf_op jit(solution)/shard_map/pallas_call | solution.py:338
  164.5 5.6 %shard_map.78 = f32[64,8192]{1,0:T(8,128)} custom-call(f32[32,64,256]{2,1,0:T(8,128)} %copy-done.2), custom_call_target="tpu_custom_call" | custom-call | tf_op jit(solution)/shard_map/pallas_call | solution.py:114
  (47 shorter events, 11.1 us)
Async XLA Ops:
  0.6 0.8 copy-start
  1.4 0.8 copy-start.1
  70.7 3.7 %copy-start.11 = (s32[4096,1]{0,1:T(1,128)S(1)}, s32[4096,1]{0,1:T(1,128)}, u32[]{:S(2)}) copy-start(s32[4096,1]{0,1:T(1,128)} %param.7) | copy-start | bytes 49156
  70.7 3.7 %copy-start.10 = (s32[4096]{0:T(1024)S(1)}, s32[4096]{0:T(1024)}, u32[]{:S(2)}) copy-start(s32[4096]{0:T(1024)} %param.8) | copy-start | bytes 49156
  70.7 92.4 %all-to-all-start.1 = ((f32[32,64,256]{2,1,0:T(8,128)}), f32[32,64,256]{2,1,0:T(8,128)S(1)}, u32[]{:S(2)}, u32[]{:S(2)}) async-start(f32[32,64,256]{2,1,0:T(8,128)} %shard_map.77), calls=%async_computation.1 | async-start | bytes 4194304 | tf_op jit(solution)/shard_map/all_to_all | solution.py:385
  83.3 2.0 %collective-permute-start = (f32[1024,128]{1,0:T(8,128)S(1)}, f32[1024,128]{1,0:T(8,128)S(1)}, u32[]{:S(2)}, u32[]{:S(2)}) collective-permute-start(f32[1024,128]{1,0:T(8,128)S(1)} %slice.41), channel_id=1, source_target_pairs={{0,1},{1,0},{2,3},{3,2},{4,5},{5,4},{6,7},{7,6},{8,9},{9,8},{10,11... | collective-permute-start | bytes 1572872 | tf_op jit(solution)/shard_map/ppermute | solution.py:351
  85.4 10.3 %collective-permute-start.1 = (f32[256,128]{1,0:T(8,128)S(1)}, f32[256,128]{1,0:T(8,128)S(1)}, u32[]{:S(2)}, u32[]{:S(2)}) collective-permute-start(f32[256,128]{1,0:T(8,128)S(1)} %get-tuple-element.11), channel_id=1, source_target_pairs={{0,4},{1,5},{2,6},{3,7},{4,0},{5,1},{6,2},{7,3},{8,12},{9,13},{10,... | collective-permute-start | bytes 393224 | tf_op jit(solution)/shard_map/ppermute | solution.py:351
  87.3 8.4 %collective-permute-start.2 = (f32[256,128]{1,0:T(8,128)S(1)}, f32[256,128]{1,0:T(8,128)S(1)}, u32[]{:S(2)}, u32[]{:S(2)}) collective-permute-start(f32[256,128]{1,0:T(8,128)S(1)} %get-tuple-element.13), channel_id=1, source_target_pairs={{0,2},{1,3},{2,0},{3,1},{4,6},{5,7},{6,4},{7,5},{8,10},{9,11},{10,... | collective-permute-start | bytes 393224 | tf_op jit(solution)/shard_map/ppermute | solution.py:351
  88.7 14.9 %collective-permute-start.3 = (f32[256,128]{1,0:T(8,128)S(1)}, f32[256,128]{1,0:T(8,128)S(1)}, u32[]{:S(2)}, u32[]{:S(2)}) collective-permute-start(f32[256,128]{1,0:T(8,128)S(1)} %get-tuple-element.12), channel_id=1, source_target_pairs={{0,6},{1,7},{2,4},{3,5},{4,2},{5,3},{6,0},{7,1},{8,14},{9,15},{10,... | collective-permute-start | bytes 393224 | tf_op jit(solution)/shard_map/ppermute | solution.py:351
  103.7 22.0 %collective-permute-start.4 = (f32[64,128]{1,0:T(8,128)S(1)}, f32[64,128]{1,0:T(8,128)S(1)}, u32[]{:S(2)}, u32[]{:S(2)}) collective-permute-start(f32[64,128]{1,0:T(8,128)S(1)} %get-tuple-element.14), channel_id=1, source_target_pairs={{0,16},{1,17},{2,18},{3,19},{4,20},{5,21},{6,22},{7,23},{8,24},{9,... | collective-permute-start | bytes 98312 | tf_op jit(solution)/shard_map/ppermute | solution.py:351
  103.7 21.9 %collective-permute-start.5 = (f32[64,128]{1,0:T(8,128)S(1)}, f32[64,128]{1,0:T(8,128)S(1)}, u32[]{:S(2)}, u32[]{:S(2)}) collective-permute-start(f32[64,128]{1,0:T(8,128)S(1)} %get-tuple-element.16), channel_id=1, source_target_pairs={{0,8},{1,9},{2,10},{3,11},{4,12},{5,13},{6,14},{7,15},{8,0},{9,1},... | collective-permute-start | bytes 98312 | tf_op jit(solution)/shard_map/ppermute | solution.py:351
  105.4 20.2 %collective-permute-start.6 = (f32[64,128]{1,0:T(8,128)S(1)}, f32[64,128]{1,0:T(8,128)S(1)}, u32[]{:S(2)}, u32[]{:S(2)}) collective-permute-start(f32[64,128]{1,0:T(8,128)S(1)} %get-tuple-element.15), channel_id=1, source_target_pairs={{0,24},{1,25},{2,26},{3,27},{4,28},{5,29},{6,30},{7,31},{8,16},{9,... | collective-permute-start | bytes 98312 | tf_op jit(solution)/shard_map/ppermute | solution.py:351
  128.2 4.4 %collective-permute-start.7 = (f32[64,128]{1,0:T(8,128)}, f32[64,128]{1,0:T(8,128)S(1)}, u32[]{:S(2)}, u32[]{:S(2)}) collective-permute-start(f32[64,128]{1,0:T(8,128)} %get-tuple-element.8.refs_0_), channel_id=1, source_target_pairs={{0,8},{1,9},{2,10},{3,11},{4,12},{5,13},{6,14},{7,15},{8,0},{9,1},... | collective-permute-start | bytes 98312 | tf_op jit(solution)/shard_map/ppermute | solution.py:351
  129.1 5.7 %collective-permute-start.8 = (f32[64,128]{1,0:T(8,128)}, f32[64,128]{1,0:T(8,128)S(1)}, u32[]{:S(2)}, u32[]{:S(2)}) collective-permute-start(f32[64,128]{1,0:T(8,128)} %get-tuple-element.8.refs_0_), channel_id=1, source_target_pairs={{0,16},{1,17},{2,18},{3,19},{4,20},{5,21},{6,22},{7,23},{8,24},{9,... | collective-permute-start | bytes 98312 | tf_op jit(solution)/shard_map/ppermute | solution.py:351
  130.0 5.9 %collective-permute-start.9 = (f32[64,128]{1,0:T(8,128)}, f32[64,128]{1,0:T(8,128)S(1)}, u32[]{:S(2)}, u32[]{:S(2)}) collective-permute-start(f32[64,128]{1,0:T(8,128)} %get-tuple-element.8.refs_0_), channel_id=1, source_target_pairs={{0,24},{1,25},{2,26},{3,27},{4,28},{5,29},{6,30},{7,31},{8,16},{9,... | collective-permute-start | bytes 98312 | tf_op jit(solution)/shard_map/ppermute | solution.py:351
  132.6 3.3 %copy-start.3 = (f32[64,128]{1,0:T(8,128)}, f32[64,128]{1,0:T(8,128)S(1)}, u32[]{:S(2)}) copy-start(f32[64,128]{1,0:T(8,128)S(1)} %collective-permute-done.7.refs_1_) | copy-start | bytes 98308
  134.9 1.1 copy-start.5
  138.1 4.1 %collective-permute-start.10 = (f32[64,128]{1,0:T(8,128)}, f32[64,128]{1,0:T(8,128)S(1)}, u32[]{:S(2)}, u32[]{:S(2)}) collective-permute-start(f32[64,128]{1,0:T(8,128)} %shard_map.81.refs_0_), channel_id=1, source_target_pairs={{0,2},{1,3},{2,0},{3,1},{4,6},{5,7},{6,4},{7,5},{8,10},{9,11},{10,... | collective-permute-start | bytes 98312 | tf_op jit(solution)/shard_map/ppermute | solution.py:351
  139.8 4.1 %collective-permute-start.11 = (f32[64,128]{1,0:T(8,128)}, f32[64,128]{1,0:T(8,128)S(1)}, u32[]{:S(2)}, u32[]{:S(2)}) collective-permute-start(f32[64,128]{1,0:T(8,128)} %shard_map.81.refs_0_), channel_id=1, source_target_pairs={{0,4},{1,5},{2,6},{3,7},{4,0},{5,1},{6,2},{7,3},{8,12},{9,13},{10,... | collective-permute-start | bytes 98312 | tf_op jit(solution)/shard_map/ppermute | solution.py:351
  141.5 5.0 %collective-permute-start.12 = (f32[64,128]{1,0:T(8,128)}, f32[64,128]{1,0:T(8,128)S(1)}, u32[]{:S(2)}, u32[]{:S(2)}) collective-permute-start(f32[64,128]{1,0:T(8,128)} %shard_map.81.refs_0_), channel_id=1, source_target_pairs={{0,6},{1,7},{2,4},{3,5},{4,2},{5,3},{6,0},{7,1},{8,14},{9,15},{10,... | collective-permute-start | bytes 98312 | tf_op jit(solution)/shard_map/ppermute | solution.py:351
  142.2 4.3 %copy-start.4 = (f32[64,128]{1,0:T(8,128)}, f32[64,128]{1,0:T(8,128)S(1)}, u32[]{:S(2)}) copy-start(f32[64,128]{1,0:T(8,128)S(1)} %collective-permute-done.10.refs_1_) | copy-start | bytes 98308
  143.9 2.6 %copy-start.6 = (f32[64,128]{1,0:T(8,128)}, f32[64,128]{1,0:T(8,128)S(1)}, u32[]{:S(2)}) copy-start(f32[64,128]{1,0:T(8,128)S(1)} %collective-permute-done.11.refs_2_) | copy-start | bytes 98308
  148.7 1.4 collective-permute-start.13
  163.2 1.3 copy-start.2
  (3 other events, 1.8 us)
